TPU v7x, 32 devices: a whole 2x2x4 slice. The times are simulated.
32 devices in a mesh: groups: 2 (over y), tm: 4 (over z), height: 4 (over x, core).
Axes of the slice: x: 2, y: 2, z: 4, core: 2. Of those that a mesh axis runs over, the one named last changes fastest.
Arguments:
- video: bfloat16 [16, 16, 64, 256], P(('groups', 'tm'), 'height'), parts along dimension 0, may hold values from -8 to 8
- norm_gain: float32 [256], replicated, may hold values from 0.25 to 1.75
- spatial_weight: bfloat16 [3, 3, 256, 256], P(None, None, 'height'), may hold values from -0.125 to 0.125
- temporal_weight: bfloat16 [3, 256, 256], replicated, may hold values from -0.21875 to 0.21875
- haar_weight: bfloat16 [2048, 512], replicated, may hold values from -0.125 to 0.125
- query_weight: bfloat16 [512, 512], replicated, may hold values from -1.5 to 1.5
- key_weight: bfloat16 [512, 512], replicated, may hold values from -1.5 to 1.5
Outputs:
- encoded: bfloat16 [8, 8, 32, 512], P(('groups', 'tm'), 'height'), parts along dimension 0
There are 2 independent parts, one for each index of `groups`. A program takes and returns all parts, laid end to end along the dimension named above; an argument that names none is the same for every part. Nothing has to cross between parts.
All inputs are finite; a program needn't handle non-finite values.
Results may differ from a plain program's by a relative error of at most 0.015.
Values may be sent and summed in bfloat16 or wider, within the bound.
A program may use at most 64 MiB of HBM per device.

v0:
```python
import jax
import jax.numpy as jnp
from jax import lax
from jax.sharding import PartitionSpec as P

HEAD_DIM = 64


epsilon = 1e-06
inv_root = 0.7071067811865476


def extended_2(x, sides, width):
    for axis, dim in sides:
        devices, length = (lax.axis_size(axis), x.shape[dim])
        up = [(i, (i + 1) % devices) for i in range(devices - 1)]
        down = [(j, i) for i, j in up]
        last = lax.slice_in_dim(x, length - width, length, axis=dim)
        initial = lax.slice_in_dim(x, 0, width, axis=dim)
        before = lax.ppermute(last, axis, up)
        after = lax.ppermute(initial, axis, down)
        x = jnp.concatenate([before, x, after], axis=dim)
    return x


def shifted(x, axis, by):
    devices = lax.axis_size(axis)
    pairs = [(i, i + by) for i in range(devices) if 0 <= i + by < devices]
    return lax.ppermute(x, axis, pairs)


def activate(video, norm_gain):
    values = video.astype(jnp.float32)
    square = jnp.mean(values * values, axis=-1, keepdims=True)
    normed = values * lax.rsqrt(square + epsilon) * norm_gain
    return (normed * jax.nn.sigmoid(normed)).astype(jnp.bfloat16)


def haar_split(values, axis_pos):
    first = lax.index_in_dim(values, 0, axis_pos, keepdims=False)
    second = lax.index_in_dim(values, 1, axis_pos, keepdims=False)
    return jnp.stack([first + second, first - second], axis=axis_pos) * inv_root


def haar_bands(merged):
    frames, rows, columns, channels = merged.shape
    values = merged.astype(jnp.float32).reshape(
        frames // 2, 2, rows // 2, 2, columns // 2, 2, channels
    )
    for axis_pos in (1, 3, 5):
        values = haar_split(values, axis_pos)
    values = jnp.transpose(values, (0, 2, 4, 1, 3, 5, 6))
    return values.reshape(frames // 2, rows // 2, columns // 2, 8 * channels).astype(jnp.bfloat16)


def causal_attention(parts):
    queries, keys, values = parts
    frames, places, width = queries.shape
    heads = width // HEAD_DIM
    query_heads = queries.reshape(frames, places, heads, HEAD_DIM)
    key_heads = keys.reshape(frames, places, heads, HEAD_DIM)
    value_heads = values.reshape(frames, places, heads, HEAD_DIM)
    scores = jnp.einsum(
        "tphd,sphd->phts", query_heads, key_heads, preferred_element_type=jnp.float32
    ) * HEAD_DIM ** (-0.5)
    order = jnp.arange(frames)
    allowed = order[None, :] <= order[:, None]
    scores = jnp.where(allowed, scores, -1e30)
    top = jnp.max(scores, axis=-1, keepdims=True)
    weights = jnp.exp(scores - top)
    probs = (weights / jnp.sum(weights, axis=-1, keepdims=True)).astype(jnp.bfloat16)
    mixed = jnp.einsum("phts,sphd->tphd", probs, value_heads, preferred_element_type=jnp.float32)
    return mixed.reshape(frames, places, width).astype(jnp.bfloat16)


def body(video, norm_gain, spatial_weight, temporal_weight, haar_weight, query_weight, key_weight):
    frames, rows, columns, channels = video.shape
    outward = spatial_weight.shape[3]
    acted = activate(video, norm_gain)
    rimmed = extended_2(acted, (("height", 1),), 1)
    padded = jnp.pad(rimmed, ((0, 0), (0, 0), (1, 1), (0, 0)))
    start_total = jnp.zeros((frames * rows * columns, outward), jnp.float32)
    total = start_total
    piece = lax.all_gather(spatial_weight, "height", axis=2, tiled=True)
    count = piece.shape[2]
    for row_tap in range(3):
        for col_tap in range(3):
            add_window = padded[
                :, row_tap : row_tap + rows, col_tap : col_tap + columns, :
            ].reshape(-1, count)
            total = total + jnp.dot(
                add_window, piece[row_tap, col_tap], preferred_element_type=jnp.float32
            )
    spatial = total.astype(jnp.bfloat16).reshape(frames, rows, columns, outward)
    earlier = shifted(spatial, "tm", 1)
    extended = jnp.concatenate([earlier, spatial], axis=0)
    temporal = jnp.zeros((frames * rows * columns, channels), jnp.float32)
    for frame_tap in range(3):
        window = extended[frame_tap : frame_tap + frames].reshape(-1, outward)
        temporal = temporal + jnp.dot(
            window, temporal_weight[frame_tap], preferred_element_type=jnp.float32
        )
    merged = (video.astype(jnp.float32).reshape(-1, channels) + temporal).astype(jnp.bfloat16)
    bands = haar_bands(merged.reshape(frames, rows, columns, channels))
    coarse_frames, coarse_rows, coarse_cols, band_width = bands.shape
    latent = jnp.dot(
        bands.reshape(-1, band_width), haar_weight, preferred_element_type=jnp.float32
    ).astype(jnp.bfloat16)
    width = latent.shape[1]
    places = coarse_rows * coarse_cols
    latent_three = latent.reshape(coarse_frames, places, width)
    members = lax.axis_size("tm")
    per_group = places // members
    grouped = latent_three.reshape(coarse_frames, members, per_group, width)
    gathered = lax.all_to_all(grouped, "tm", split_axis=1, concat_axis=0, tiled=True)
    all_frames, single, count, depth = gathered.shape
    flat_latent = gathered.reshape(-1, depth)
    group_queries = jnp.dot(flat_latent, query_weight, preferred_element_type=jnp.float32).astype(
        jnp.bfloat16
    )
    group_keys = jnp.dot(flat_latent, key_weight, preferred_element_type=jnp.float32).astype(
        jnp.bfloat16
    )
    shaped = tuple(
        (
            item.reshape(all_frames, single * count, depth)
            for item in (group_queries, group_keys, flat_latent)
        )
    )
    mixed_group = causal_attention(shaped)
    regrouped = mixed_group.reshape(all_frames, single, count, depth)
    returned = lax.all_to_all(regrouped, "tm", split_axis=0, concat_axis=1, tiled=True)
    mixed = returned.reshape(coarse_frames, places, width)
    result = (latent_three.astype(jnp.float32) + mixed.astype(jnp.float32)).astype(jnp.bfloat16)
    return result.reshape(coarse_frames, coarse_rows, coarse_cols, width)


def solution(mesh):
    in_specs = (
        P(("groups", "tm"), "height", None, None),
        P(),
        P(None, None, "height", None),
        P(),
        P(),
        P(),
        P(),
    )
    out_specs = P(("groups", "tm"), "height", None, None)
    return jax.shard_map(body, mesh=mesh, in_specs=in_specs, out_specs=out_specs, check_vma=False)
```

profile of v0, /device:TPU:0, one launch (start us, length us, event | category | flops | bytes accessed | tf_op | source)
XLA Modules:
  0.0 78.3 jit_solution(16204435591119110432)
XLA Ops:
  6.5 0.0 copy-start
  6.5 0.0 all-gather.2.cloned.1.call-start
  6.5 0.7 all-gather.2.cloned.1.call-update
  7.3 1.1 %multiply_reduce_fusion = f32[2,4,64]{2,1,0:T(4,128)S(1)} fusion(bf16[2,4,64,256]{3,2,1,0:T(8,128)(2,1)} %param.7), kind=kLoop, calls=%fused_computation.27 | loop fusion | flops 392704 | bytes 264192 | tf_op jit(solution)/shard_map/reduce_sum | solution.py:34
  8.4 1.2 %multiply_convert_fusion = bf16[2,4,64,256]{3,2,1,0:T(8,128)(2,1)S(1)} fusion(f32[256]{0:T(256)} %param.8, f32[2,4,64]{2,1,0:T(4,128)S(1)} %add_rsqrt_fusion, bf16[2,4,64,256]{3,2,1,0:T(8,128)(2,1)} %param.7), kind=kLoop, calls=%fused_computation.26 | loop fusion | flops 1048576 | bytes 527360 | tf_op jit(solution)/shard_map/convert_element_type | solution.py:36
  9.6 2.4 %collective-permute-start = (bf16[2,1,64,256]{3,2,1,0:T(8,128)(2,1)S(1)}, bf16[2,1,64,256]{3,2,1,0:T(8,128)(2,1)S(1)}, u32[]{:S(2)}, u32[]{:S(2)}) collective-permute-start(bf16[2,1,64,256]{3,2,1,0:T(8,128)(2,1)S(1)} %get-tuple-element.21), channel_id=1, source_target_pairs={{0,1},{1,2},{2,3},{4,5},{5,6},{6,7},{8,9},{9,10},{10,11},{12,13},{... | collective-permute-start | bytes 196616 | tf_op jit(solution)/shard_map/ppermute | solution.py:20
  12.0 1.3 %collective-permute-start.1 = (bf16[2,1,64,256]{3,2,1,0:T(8,128)(2,1)S(1)}, bf16[2,1,64,256]{3,2,1,0:T(8,128)(2,1)S(1)}, u32[]{:S(2)}, u32[]{:S(2)}) collective-permute-start(bf16[2,1,64,256]{3,2,1,0:T(8,128)(2,1)S(1)} %get-tuple-element.22), channel_id=1, source_target_pairs={{1,0},{2,1},{3,2},{5,4},{6,5},{7,6},{9,8},{10,9},{11,10},{13,12},{... | collective-permute-start | bytes 196616 | tf_op jit(solution)/shard_map/ppermute | solution.py:21
  13.3 0.0 collective-permute-done
  13.3 3.9 %collective-permute-done.1 = bf16[2,1,64,256]{3,2,1,0:T(8,128)(2,1)S(1)} collective-permute-done((bf16[2,1,64,256]{3,2,1,0:T(8,128)(2,1)S(1)}, bf16[2,1,64,256]{3,2,1,0:T(8,128)(2,1)S(1)}, u32[]{:S(2)}, u32[]{:S(2)}) %collective-permute-start.1) | collective-permute-done | bytes 65568 | tf_op jit(solution)/shard_map/ppermute | solution.py:21
  17.2 0.1 fusion.13
  17.3 0.7 pad_maximum_fusion.1
  18.1 1.0 %fusion.33 = (bf16[2,4,64,256]{3,2,1,0:T(8,128)(2,1)S(1)}, bf16[2,4,64,256]{3,2,1,0:T(8,128)(2,1)}, bf16[2,4,64,256]{3,2,1,0:T(8,128)(2,1)}, bf16[2,4,64,256]{3,...) fusion(bf16[2,6,66,256]{3,2,1,0:T(8,128)(2,1)S(1)} %fusion.13), kind=kLoop, calls=%fused_computation.76 | loop fusion | bytes 3145728 | tf_op jit(solution)/shard_map/slice | solution.py:88
  19.1 10.0 %all-gather.2.cloned.1.call-done = bf16[3,3,256,256]{3,2,1,0:T(8,128)(2,1)} async-done(((bf16[3,3,64,256]{3,2,1,0:T(8,128)(2,1)}), bf16[3,3,256,256]{3,2,1,0:T(8,128)(2,1)}) %all-gather.2.cloned.1.call-update) | async-done | bytes 1179664 | tf_op jit(solution)/shard_map/all_gather | solution.py:84
  29.1 1.2 %fusion.16 = f32[512,256]{1,0:T(8,128)S(1)} fusion(bf16[512,256]{1,0:T(8,128)(2,1)S(1)} %bitcast.93, bf16[3,3,256,256]{3,2,1,0:T(8,128)(2,1)} %all-gather.2.cloned.1.call-done), kind=kOutput, calls=%fused_computation.53 | convolution fusion | flops 67108864 | bytes 917504 | tf_op jit(solution)/shard_map/dot_general | solution.py:91
  30.4 0.0 copy-start.6
  30.4 1.2 %fusion.15 = f32[512,256]{1,0:T(8,128)S(1)} fusion(bf16[512,256]{1,0:T(8,128)(2,1)S(1)} %bitcast.92, bf16[3,3,256,256]{3,2,1,0:T(8,128)(2,1)} %all-gather.2.cloned.1.call-done), kind=kOutput, calls=%fused_computation.44 | convolution fusion | flops 67108864 | bytes 917504 | tf_op jit(solution)/shard_map/dot_general | solution.py:91
  31.5 0.0 copy-done.2
  31.6 0.2 convolution_add_fusion.7
  31.8 0.0 copy-done.6
  31.8 0.2 convolution_add_fusion.6
  32.0 0.5 copy-done.5
  32.5 0.2 convolution_add_fusion.5
  32.7 0.2 convolution_add_fusion.4
  33.0 0.5 copy-done.3
  33.5 0.2 convolution_add_fusion.3
  33.7 0.2 convolution_add_fusion.2
  33.9 0.0 copy-start.9
  33.9 0.2 fusion.5
  34.2 0.0 copy-start.1
  34.2 3.5 %collective-permute-start.2 = (bf16[2,4,64,256]{3,2,1,0:T(8,128)(2,1)S(1)}, bf16[2,4,64,256]{3,2,1,0:T(8,128)(2,1)S(1)}, u32[]{:S(2)}, u32[]{:S(2)}) collective-permute-start(bf16[2,4,64,256]{3,2,1,0:T(8,128)(2,1)S(1)} %bitcast.90), channel_id=1, source_target_pairs={{0,4},{4,8},{8,12},{1,5},{5,9},{9,13},{2,6},{6,10},{10,14},{3,7},{... | collective-permute-start | bytes 786440 | tf_op jit(solution)/shard_map/ppermute | solution.py:29
  37.7 0.2 fusion.18
  38.0 5.7 %collective-permute-done.2 = bf16[2,4,64,256]{3,2,1,0:T(8,128)(2,1)S(1)} collective-permute-done((bf16[2,4,64,256]{3,2,1,0:T(8,128)(2,1)S(1)}, bf16[2,4,64,256]{3,2,1,0:T(8,128)(2,1)S(1)}, u32[]{:S(2)}, u32[]{:S(2)}) %collective-permute-start.2) | collective-permute-done | bytes 262176 | tf_op jit(solution)/shard_map/ppermute | solution.py:29
  43.7 0.2 fusion.20
  43.9 0.2 fusion.4
  44.2 0.3 reshape.239
  44.5 0.2 fusion.32
  44.7 0.2 copy_add_fusion
  44.9 0.3 maximum_multiply_fusion
  45.2 0.2 slice_add_fusion
  45.4 0.3 maximum_multiply_fusion.1
  45.7 0.4 slice_add_fusion.1
  46.1 0.6 fusion.14
  46.7 0.2 convert_element_type.91
  46.9 0.0 copy-done
  46.9 0.0 copy-start.7
  46.9 0.0 copy-start.8
  46.9 1.1 %convolution_convert_fusion.3 = bf16[64,512]{1,0:T(8,128)(2,1)} fusion(bf16[64,2048]{1,0:T(8,128)(2,1)S(1)} %convert_element_type.91, bf16[2048,512]{1,0:T(8,128)(2,1)S(1)} %copy-done), kind=kOutput, calls=%fused_computation.20 | convolution fusion | flops 134250496 | bytes 2424832 | tf_op jit(solution)/shard_map/dot_general | solution.py:106
  48.0 5.6 %all-to-all-start = ((bf16[1,4,16,512]{3,2,0,1:T(8,128)(2,1)}), bf16[1,4,16,512]{3,2,0,1:T(8,128)(2,1)S(1)}, u32[]{:S(2)}, u32[]{:S(2)}) async-start(bf16[1,4,16,512]{3,2,0,1:T(8,128)(2,1)} %bitcast.27), calls=%async_computation | async-start | bytes 131072 | tf_op jit(solution)/shard_map/all_to_all | solution.py:115
  53.6 5.7 %all-to-all-done = bf16[1,4,16,512]{3,2,0,1:T(8,128)(2,1)S(1)} async-done(((bf16[1,4,16,512]{3,2,0,1:T(8,128)(2,1)}), bf16[1,4,16,512]{3,2,0,1:T(8,128)(2,1)S(1)}, u32[]{:S(2)}, u32[]{:S(2)}) %all-to-all-start) | async-done | bytes 65568 | tf_op jit(solution)/shard_map/all_to_all | solution.py:115
  59.4 0.2 convolution_convert_fusion.2
  59.6 0.1 reshape_reshape.10
  59.7 0.2 convolution_convert_fusion.1
  59.9 0.1 reshape_reshape.11
  60.0 0.3 fusion.24
  60.3 0.3 copy.32
  60.7 0.1 fusion.30
  60.8 0.1 fusion.31
  60.9 0.1 divide_convert_fusion
  61.0 0.3 copy.34
  61.3 0.1 reshape_reshape_reshape.3
  61.4 0.3 fusion.6
  61.8 0.1 convert_element_type.99
  61.9 8.1 %all_to_all.8 = bf16[4,1,16,512]{3,2,1,0:T(8,128)(2,1)S(1)} all-to-all(bf16[4,1,16,512]{3,2,1,0:T(8,128)(2,1)S(1)} %bitcast.104), channel_id=1, replica_groups=mesh['groups'=2,'tm'=4,'height'=4] {'tm'}, dimensions={0} | all-to-all | bytes 131072 | tf_op jit(solution)/shard_map/all_to_all | solution.py:132
  70.0 1.5 %fusion.17 = bf16[64,512]{1,0:T(8,128)(2,1)} fusion(bf16[64,512]{1,0:T(8,128)(2,1)} %convolution_convert_fusion.3, bf16[4,1,16,512]{3,2,1,0:T(8,128)(2,1)S(1)} %all_to_all.8), kind=kLoop, calls=%fused_computation.55 | loop fusion | flops 131072 | bytes 196608 | tf_op jit(solution)/shard_map/convert_element_type | solution.py:134
  (14 shorter events, 0.1 us)
Async XLA Ops:
  6.5 40.3 %copy-start = (bf16[2048,512]{1,0:T(8,128)(2,1)S(1)}, bf16[2048,512]{1,0:T(8,128)(2,1)}, u32[]{:S(2)}) copy-start(bf16[2048,512]{1,0:T(8,128)(2,1)} %param.11) | copy-start | bytes 6291460
  6.5 22.6 %all-gather.2.cloned.1.call-start = ((), (), s32[]{:S(2)}) async-start(), calls=%async_computation.2 | async-start | bytes 1474560 | tf_op jit(solution)/shard_map/all_gather | solution.py:84
  9.6 3.7 %collective-permute-start = (bf16[2,1,64,256]{3,2,1,0:T(8,128)(2,1)S(1)}, bf16[2,1,64,256]{3,2,1,0:T(8,128)(2,1)S(1)}, u32[]{:S(2)}, u32[]{:S(2)}) collective-permute-start(bf16[2,1,64,256]{3,2,1,0:T(8,128)(2,1)S(1)} %get-tuple-element.21), channel_id=1, source_target_pairs={{0,1},{1,2},{2,3},{4,5},{5,6},{6,7},{8,9},{9,10},{10,11},{12,13},{... | collective-permute-start | bytes 196616 | tf_op jit(solution)/shard_map/ppermute | solution.py:20
  12.0 5.3 %collective-permute-start.1 = (bf16[2,1,64,256]{3,2,1,0:T(8,128)(2,1)S(1)}, bf16[2,1,64,256]{3,2,1,0:T(8,128)(2,1)S(1)}, u32[]{:S(2)}, u32[]{:S(2)}) collective-permute-start(bf16[2,1,64,256]{3,2,1,0:T(8,128)(2,1)S(1)} %get-tuple-element.22), channel_id=1, source_target_pairs={{1,0},{2,1},{3,2},{5,4},{6,5},{7,6},{9,8},{10,9},{11,10},{13,12},{... | collective-permute-start | bytes 196616 | tf_op jit(solution)/shard_map/ppermute | solution.py:21
  29.1 2.4 %copy-start.2 = (bf16[3,3,256,256]{3,2,1,0:T(8,128)(2,1)S(1)}, bf16[3,3,256,256]{3,2,1,0:T(8,128)(2,1)}, u32[]{:S(2)}) copy-start(bf16[3,3,256,256]{3,2,1,0:T(8,128)(2,1)} %all-gather.2.cloned.1.call-done) | copy-start | bytes 3538948
  29.1 2.4 %copy-start.4 = (bf16[2,4,64,256]{3,2,1,0:T(8,128)(2,1)S(1)}, bf16[2,4,64,256]{3,2,1,0:T(8,128)(2,1)}, u32[]{:S(2)}) copy-start(bf16[2,4,64,256]{3,2,1,0:T(8,128)(2,1)} %get-tuple-element.20) | copy-start | bytes 786436
  30.4 1.4 %copy-start.6 = (bf16[2,4,64,256]{3,2,1,0:T(8,128)(2,1)S(1)}, bf16[2,4,64,256]{3,2,1,0:T(8,128)(2,1)}, u32[]{:S(2)}) copy-start(bf16[2,4,64,256]{3,2,1,0:T(8,128)(2,1)} %get-tuple-element.16) | copy-start | bytes 786436
  31.6 1.0 %copy-start.5 = (bf16[2,4,64,256]{3,2,1,0:T(8,128)(2,1)S(1)}, bf16[2,4,64,256]{3,2,1,0:T(8,128)(2,1)}, u32[]{:S(2)}) copy-start(bf16[2,4,64,256]{3,2,1,0:T(8,128)(2,1)} %get-tuple-element.15) | copy-start | bytes 786436
  32.5 0.9 %copy-start.3 = (bf16[2,4,64,256]{3,2,1,0:T(8,128)(2,1)S(1)}, bf16[2,4,64,256]{3,2,1,0:T(8,128)(2,1)}, u32[]{:S(2)}) copy-start(bf16[2,4,64,256]{3,2,1,0:T(8,128)(2,1)} %get-tuple-element.14) | copy-start | bytes 786436
  33.9 3.8 %copy-start.9 = (bf16[3,256,256]{2,1,0:T(8,128)(2,1)S(1)}, bf16[3,256,256]{2,1,0:T(8,128)(2,1)}, u32[]{:S(2)}) copy-start(bf16[3,256,256]{2,1,0:T(8,128)(2,1)} %param.10) | copy-start | bytes 1179652
  34.2 9.7 %copy-start.1 = (bf16[2,4,64,256]{3,2,1,0:T(8,128)(2,1)S(1)}, bf16[2,4,64,256]{3,2,1,0:T(8,128)(2,1)}, u32[]{:S(2)}) copy-start(bf16[2,4,64,256]{3,2,1,0:T(8,128)(2,1)} %param.7) | copy-start | bytes 786436
  34.2 9.5 %collective-permute-start.2 = (bf16[2,4,64,256]{3,2,1,0:T(8,128)(2,1)S(1)}, bf16[2,4,64,256]{3,2,1,0:T(8,128)(2,1)S(1)}, u32[]{:S(2)}, u32[]{:S(2)}) collective-permute-start(bf16[2,4,64,256]{3,2,1,0:T(8,128)(2,1)S(1)} %bitcast.90), channel_id=1, source_target_pairs={{0,4},{4,8},{8,12},{1,5},{5,9},{9,13},{2,6},{6,10},{10,14},{3,7},{... | collective-permute-start | bytes 786440 | tf_op jit(solution)/shard_map/ppermute | solution.py:29
  46.9 12.5 %copy-start.7 = (bf16[512,512]{1,0:T(8,128)(2,1)S(1)}, bf16[512,512]{1,0:T(8,128)(2,1)}, u32[]{:S(2)}) copy-start(bf16[512,512]{1,0:T(8,128)(2,1)} %param.12) | copy-start | bytes 1572868
  46.9 12.8 %copy-start.8 = (bf16[512,512]{1,0:T(8,128)(2,1)S(1)}, bf16[512,512]{1,0:T(8,128)(2,1)}, u32[]{:S(2)}) copy-start(bf16[512,512]{1,0:T(8,128)(2,1)} %param.13) | copy-start | bytes 1572868
  48.0 11.3 %all-to-all-start = ((bf16[1,4,16,512]{3,2,0,1:T(8,128)(2,1)}), bf16[1,4,16,512]{3,2,0,1:T(8,128)(2,1)S(1)}, u32[]{:S(2)}, u32[]{:S(2)}) async-start(bf16[1,4,16,512]{3,2,0,1:T(8,128)(2,1)} %bitcast.27), calls=%async_computation | async-start | bytes 131072 | tf_op jit(solution)/shard_map/all_to_all | solution.py:115
Sparse Core Ops, SparseCore 0:
  8.9 20.1 all-gather.1
where the time goes:
time: 78.8 us; the launch traced here: 78.3 us
  waiting for transfers between devices  26.1 us (33%)
  between operations  13.8 us (18%)
  starting transfers between devices  12.8 us (16%)
  blocking collectives  8.11 us (10%)
  other arithmetic  6.94 us (9%)
  matrix products  6.72 us (9%)
  local copies, waits for them, and re-layouts  3.92 us (5%)
    all_gather x1, waiting for transfers between devices, body(): piece = lax.all_gather(spatial_weight, 'height', axis=2, tiled=True)  10 us
    all_to_all x1, blocking collectives, body(): lax.all_to_all(regrouped, 'tm', split_axis=0, concat_axis=1, tiled=True)  8.11 us
    all_to_all x1, waiting for transfers between devices, body(): lax.all_to_all(grouped, 'tm', split_axis=1, concat_axis=0, tiled=True)  5.74 us
    ppermute x1, waiting for transfers between devices, shifted(): return lax.ppermute(x, axis, pairs)  5.69 us
    all_to_all x1, starting transfers between devices, body(): lax.all_to_all(grouped, 'tm', split_axis=1, concat_axis=0, tiled=True)  5.6 us
    dot_general x9, matrix products, body(): jnp.dot(add_window, piece[row_tap, col_tap], preferred_element_type=jnp.f...  3.97 us
    ppermute x1, waiting for transfers between devices, extended_2(): after = lax.ppermute(initial, axis, down)  3.94 us
    ppermute x1, starting transfers between devices, shifted(): return lax.ppermute(x, axis, pairs)  3.54 us
  transfers between devices with their start and end apart: 5, of which 4 were waited for; matrix products, arithmetic and copies ran while one was open for 6% of the time, Pallas kernels for 0%

commit v1 on v0

v1 whole, which is shorter than its diff:
```python
import functools

import jax
import jax.numpy as jnp
import numpy as np
from jax import lax
from jax.experimental import pallas as pl
from jax.experimental.pallas import tpu as pltpu
from jax.sharding import PartitionSpec as P

HEAD_DIM = 64
epsilon = 1e-06
inv_root = 0.7071067811865476
MESH = pl.DeviceIdType.MESH


def haar_matrix(cols):
    half = cols // 2
    band = np.arange(4 * cols)[:, None] // half
    place = np.arange(4 * cols)[:, None] % half
    item = np.arange(4 * cols)[None, :]
    frame, row, col = item // (2 * cols), (item // cols) % 2, item % cols
    odd = (band // 4) * frame + ((band // 2) % 2) * row + (band % 2) * (col % 2)
    return np.where(col // 2 == place, np.where(odd % 2 == 1, -1.0, 1.0), 0.0)


def kernel(
    nh, nt, video, gain, sw, tw, hw, qw, kw, haar, heads, out,
    vid, wfull, twv, hwv, qwv, kwv, haarv, headsv, patches, acc, sp, mg, bands, gl, sc,
    local_sem, wsend, wrecv, fsend, frecv, hsend, hrecv, gsend, grecv, vsend, vrecv, lsend, lrecv,
):
    h, t = lax.axis_index("height"), lax.axis_index("tm")
    frames, rows, cols, chan = video.shape
    cin = sw.shape[2]
    chips = nh // 2
    chip, core = lax.div(h, 2), lax.rem(h, 2)
    sibling = chip * 2 + 1 - core
    f32, bf16 = jnp.float32, jnp.bfloat16

    def remote(src, dst, send, recv, **where):
        return pltpu.make_async_remote_copy(
            src_ref=src, dst_ref=dst, send_sem=send, recv_sem=recv, device_id=where, device_id_type=MESH
        )

    own_in = pl.ds(pl.multiple_of(h * cin, cin), cin)
    local = [
        pltpu.make_async_copy(video, vid.at[pl.ds(2, frames), pl.ds(1, rows)], local_sem.at[0]),
        pltpu.make_async_copy(sw, wfull.at[:, :, own_in, :], local_sem.at[1]),
        pltpu.make_async_copy(tw, twv, local_sem.at[2]),
        pltpu.make_async_copy(haar, haarv, local_sem.at[3]),
        pltpu.make_async_copy(hw, hwv, local_sem.at[4]),
        pltpu.make_async_copy(qw, qwv, local_sem.at[5]),
        pltpu.make_async_copy(kw, kwv, local_sem.at[6]),
        pltpu.make_async_copy(heads, headsv, local_sem.at[7]),
    ]
    for copy in local:
        copy.start()

    barrier = pltpu.get_barrier_semaphore()
    for d in range(1, nh):
        pl.semaphore_signal(barrier, inc=1, device_id={"height": lax.rem(h + d, nh)}, device_id_type=MESH)
    for d in range(1, nt):
        pl.semaphore_signal(barrier, inc=1, device_id={"tm": lax.rem(t + d, nt)}, device_id_type=MESH)

    total = frames + 2
    for edge, slot in ((0, 0), (nh - 1, rows + 1)):
        @pl.when(h == edge)
        def _():
            vid[:, slot] = jnp.zeros((total, cols, chan), bf16)

    @pl.when(t == 0)
    def _():
        for f in range(2):
            vid[f] = jnp.zeros((rows + 2, cols, chan), bf16)

    for d in range(1, nt):
        @pl.when(t < d)
        def _():
            gl[d] = jnp.zeros(gl.shape[1:], bf16)

    pl.semaphore_wait(barrier, nh - 1 + nt - 1)

    later = {"tm": lax.rem(t + 1, nt)}
    above, below = {"height": lax.rem(h + nh - 1, nh)}, {"height": lax.rem(h + 1, nh)}
    tail = video.at[pl.ds(frames - 2, 2)]
    mine = pl.ds(2, frames)
    halo = [
        remote(video.at[:, 0], vid.at[mine, rows + 1], hsend.at[0], hrecv.at[0], **above),
        remote(video.at[:, rows - 1], vid.at[mine, 0], hsend.at[1], hrecv.at[1], **below),
    ]
    past = [
        remote(tail.at[:, 0], vid.at[pl.ds(0, 2), 1], vsend.at[0], vrecv.at[0], **later),
        remote(tail.at[:, rows - 1], vid.at[pl.ds(0, 2), rows], vsend.at[1], vrecv.at[1], **later),
        remote(
            tail.at[:, pl.ds(1, rows - 2)], vid.at[pl.ds(0, 2), pl.ds(2, rows - 2)],
            vsend.at[2], vrecv.at[2], **later,
        ),
    ]
    relay = [
        remote(vid.at[pl.ds(0, 2), 1], vid.at[pl.ds(0, 2), rows + 1], gsend.at[0], grecv.at[0], **above),
        remote(vid.at[pl.ds(0, 2), rows], vid.at[pl.ds(0, 2), 0], gsend.at[1], grecv.at[1], **below),
    ]
    up, down, has_past, has_next = h > 0, h < nh - 1, t > 0, t < nt - 1
    sends = (up, down)
    receives = (down, up)

    weights, onward = {}, {}
    for a in range(3):
        piece = wfull.at[a, :, own_in, :]
        weights[0, a] = remote(
            sw.at[a], piece, wsend.at[0, a], wrecv.at[0, a], height=sibling
        )
        for d in range(1, chips):
            weights[d, a] = remote(
                sw.at[a], piece, wsend.at[d, a], wrecv.at[d, a],
                height=lax.rem(chip + d, chips) * 2 + core,
            )
            origin = lax.rem(chip + chips - d, chips) * 2 + core
            held = wfull.at[a, :, pl.ds(pl.multiple_of(origin * cin, cin), cin), :]
            onward[d, a] = remote(held, held, fsend.at[d, a], frecv.at[d, a], height=sibling)

    for cond, copy in zip(sends, halo):
        pl.when(cond)(copy.start)
    for copy in past:
        pl.when(has_next)(copy.start)
    for a in range(3):
        for d in range(1, chips):
            weights[d, a].start()
        weights[0, a].start()

    column = lax.broadcasted_iota(jnp.int32, (cols, chan), 0)
    scale = gain[...]

    def activate(f, r):
        values = vid[f, r].astype(f32)
        square = jnp.mean(values * values, axis=-1, keepdims=True)
        normed = values * lax.rsqrt(square + epsilon) * scale
        acted = normed * jax.nn.sigmoid(normed)
        before = jnp.where(column == 0, 0.0, pltpu.roll(acted, 1, 0))
        after = jnp.where(column == cols - 1, 0.0, pltpu.roll(acted, cols - 1, 0))
        patches[f, r, :, pl.ds(0, chan)] = before.astype(bf16)
        patches[f, r, :, pl.ds(chan, chan)] = acted.astype(bf16)
        patches[f, r, :, pl.ds(2 * chan, chan)] = after.astype(bf16)

    def activate_rows(first, count, row, height):
        def step(i, carry):
            activate(first + lax.div(i, height), row + lax.rem(i, height))
            return carry
        lax.fori_loop(0, count * height, step, 0)

    def receive(copies):
        for copy in copies:
            copy.wait_recv()

    local[0].wait()
    activate_rows(2, frames, 1, rows)
    for i in range(2):
        pl.when(has_past)(past[i].wait_recv)
        pl.when(has_past & sends[i])(relay[i].start)
    for i, row in ((0, rows + 1), (1, 0)):
        pl.when(receives[i])(halo[i].wait_recv)
        activate_rows(2, frames, row, 1)
    for d in range(1, chips):
        weights[d, 0].wait_recv()
        onward[d, 0].start()
    pl.when(has_past)(past[2].wait_recv)
    activate_rows(0, 2, 1, rows)
    for d in range(1, chips):
        weights[d, 1].wait_recv()
        onward[d, 1].start()
    for i, row in ((0, rows + 1), (1, 0)):
        pl.when(has_past & receives[i])(relay[i].wait_recv)
        activate_rows(0, 2, row, 1)
    local[1].wait()
    for a in range(3):
        if a == 1:
            for d in range(1, chips):
                weights[d, 2].wait_recv()
                onward[d, 2].start()
        weights[0, a].wait_recv()
        receive([onward[d, a] for d in range(1, chips)])
        taps = wfull[a].reshape(3 * chan, wfull.shape[3])
        for f in range(total):
            part = jnp.dot(
                patches[f, a : a + rows].reshape(rows * cols, 3 * chan), taps,
                preferred_element_type=f32,
            )
            if a == 0:
                acc[f] = part
            elif a == 1:
                acc[f] += part
            else:
                sp[f] = (acc[f] + part).astype(bf16)

    local[2].wait()
    for f in range(frames):
        temporal = jnp.dot(sp[f], twv[0], preferred_element_type=f32)
        for k in (1, 2):
            temporal += jnp.dot(sp[f + k], twv[k], preferred_element_type=f32)
        own = vid[f + 2, 1 : rows + 1].reshape(rows * cols, chan).astype(f32)
        mg[f] = (own + temporal).astype(bf16)

    local[3].wait()
    half = cols // 2
    for j in range(rows // 2):
        pair = pl.ds(2 * j * cols, 2 * cols)
        block = jnp.concatenate([mg[0, pair], mg[1, pair]], axis=0)
        split = jnp.dot(haarv[...], block, preferred_element_type=f32) * (inv_root * inv_root * inv_root)
        for band in range(8):
            bands[pl.ds(j * half, half), pl.ds(band * chan, chan)] = split[
                band * half : (band + 1) * half
            ].astype(bf16)
    local[4].wait()
    latent = jnp.dot(bands[...], hwv[...], preferred_element_type=f32).astype(bf16)
    gl[0] = latent

    shares = [None]
    for d in range(1, nt):
        shares.append(
            remote(gl.at[0], gl.at[d], lsend.at[d], lrecv.at[d], tm=lax.rem(t + d, nt))
        )
    for d in range(1, nt):
        pl.when(t + d < nt)(shares[d].start)

    local[5].wait()
    local[6].wait()
    local[7].wait()
    queries = jnp.dot(latent, qwv[...], preferred_element_type=f32).astype(bf16).astype(f32)
    width = latent.shape[1]
    group = headsv.shape[0]
    for d in range(nt):
        if d:
            pl.when(t >= d)(shares[d].wait_recv)
        keys = jnp.dot(gl[d], kwv[...], preferred_element_type=f32).astype(bf16).astype(f32)
        product = queries * keys
        high = product.astype(bf16)
        low = (product - high.astype(f32)).astype(bf16)
        for c in range(width // group):
            part = slice(c * group, (c + 1) * group)
            score = jnp.dot(high[:, part], headsv[...], preferred_element_type=f32)
            score += jnp.dot(low[:, part], headsv[...], preferred_element_type=f32)
            score = score * HEAD_DIM ** (-0.5)
            sc[d, :, part] = score if d == 0 else jnp.where(t >= d, score, -1e30)
    top = sc[0]
    for d in range(1, nt):
        top = jnp.maximum(top, sc[d])
    denominator = jnp.zeros_like(top)
    for d in range(nt):
        weight = jnp.exp(sc[d] - top)
        sc[d] = weight
        denominator += weight
    mixed = jnp.zeros_like(top)
    for d in range(nt):
        mixed += (sc[d] / denominator).astype(bf16).astype(f32) * gl[d].astype(f32)
    result = latent.astype(f32) + mixed.astype(bf16).astype(f32)
    out[...] = result.astype(bf16).reshape(out.shape)

    for i in range(2):
        pl.when(sends[i])(halo[i].wait_send)
        pl.when(has_past & sends[i])(relay[i].wait_send)
    for copy in past:
        pl.when(has_next)(copy.wait_send)
    for copy in list(weights.values()) + list(onward.values()):
        copy.wait_send()
    for d in range(1, nt):
        pl.when(t + d < nt)(shares[d].wait_send)


def body(nh, nt, video, norm_gain, sw, tw, hw, qw, kw):
    frames, rows, cols, chan = video.shape
    outward, width = sw.shape[3], hw.shape[1]
    bf16, f32 = jnp.bfloat16, jnp.float32
    group = min(256, width)
    ids = np.arange(group) // HEAD_DIM
    heads = jnp.asarray(ids[:, None] == ids[None, :], bf16)
    haar = jnp.asarray(haar_matrix(cols), bf16)
    total, places = frames + 2, rows // 2 * (cols // 2)
    dma = pltpu.SemaphoreType.DMA
    anywhere, vmem = pl.BlockSpec(memory_space=pl.ANY), pl.BlockSpec(memory_space=pltpu.VMEM)
    return pl.pallas_call(
        functools.partial(kernel, nh, nt),
        out_shape=jax.ShapeDtypeStruct((frames // 2, rows // 2, cols // 2, width), bf16),
        in_specs=[anywhere, vmem] + [anywhere] * 7,
        out_specs=vmem,
        scratch_shapes=[
            pltpu.VMEM((total, rows + 2, cols, chan), bf16),
            pltpu.VMEM((3, 3, chan, outward), bf16),
            pltpu.VMEM(tw.shape, bf16),
            pltpu.VMEM(hw.shape, bf16),
            pltpu.VMEM(qw.shape, bf16),
            pltpu.VMEM(kw.shape, bf16),
            pltpu.VMEM(haar.shape, bf16),
            pltpu.VMEM(heads.shape, bf16),
            pltpu.VMEM((total, rows + 2, cols, 3 * chan), bf16),
            pltpu.VMEM((total, rows * cols, outward), f32),
            pltpu.VMEM((total, rows * cols, outward), bf16),
            pltpu.VMEM((frames, rows * cols, chan), bf16),
            pltpu.VMEM((places, 8 * chan), bf16),
            pltpu.VMEM((nt, places, width), bf16),
            pltpu.VMEM((nt, places, width), f32),
            dma((8,)),
            dma((nh // 2, 3)), dma((nh // 2, 3)), dma((nh // 2, 3)), dma((nh // 2, 3)),
            dma((2,)), dma((2,)), dma((2,)), dma((2,)), dma((3,)), dma((3,)),
            dma((nt,)), dma((nt,)),
        ],
        compiler_params=pltpu.CompilerParams(
            collective_id=0, has_side_effects=True, vmem_limit_bytes=40 * 1024 * 1024
        ),
        cost_estimate=pl.CostEstimate(
            flops=2 * 10**9, bytes_accessed=5 * 10**6, transcendentals=10**6
        ),
    )(video, norm_gain.reshape(1, chan), sw, tw, hw, qw, kw, haar, heads)


def solution(mesh):
    in_specs = (
        P(("groups", "tm"), "height", None, None),
        P(),
        P(None, None, "height", None),
        P(),
        P(),
        P(),
        P(),
    )
    out_specs = P(("groups", "tm"), "height", None, None)
    run = functools.partial(body, mesh.shape["height"], mesh.shape["tm"])
    return jax.shard_map(run, mesh=mesh, in_specs=in_specs, out_specs=out_specs, check_vma=False)
```

time: 78.8 us -> 34.3 us (0.44)
  the two profiles are of different devices: /device:TPU:0 before, /device:TPU:28 now
where the time goes in v1:
time: 34.3 us; the launch traced here: 33.9 us
  Pallas kernels  24.1 us (70%)
  local copies, waits for them, and re-layouts  9.7 us (28%)
    pallas_call x1, Pallas kernels, body(): pl.pallas_call(functools.partial(kernel, nh, nt), out_shape=jax.ShapeDtyp...  24.1 us
    unnamed x19, local copies, waits for them, and re-layouts  9.7 us

profile of v1, /device:TPU:28, one launch (start us, length us, event | category | flops | bytes accessed | tf_op | source)
XLA Modules:
  0.0 33.9 jit_solution(11454425132726354579)
XLA Ops:
  0.0 0.0 copy-start
  0.0 1.6 %copy-done = bf16[2048,512]{1,0:T(8,128)(2,1)S(1)} copy-done((bf16[2048,512]{1,0:T(8,128)(2,1)S(1)}, bf16[2048,512]{1,0:T(8,128)(2,1)}, u32[]{:S(2)}) %copy-start) | copy-done | bytes 2097176
  1.6 0.0 copy-start.1
  1.6 1.0 %copy-done.1 = bf16[512,512]{1,0:T(8,128)(2,1)S(1)} copy-done((bf16[512,512]{1,0:T(8,128)(2,1)S(1)}, bf16[512,512]{1,0:T(8,128)(2,1)}, u32[]{:S(2)}) %copy-start.1) | copy-done | bytes 524312
  2.6 0.0 copy-start.2
  2.6 1.0 %copy-done.2 = bf16[512,512]{1,0:T(8,128)(2,1)S(1)} copy-done((bf16[512,512]{1,0:T(8,128)(2,1)S(1)}, bf16[512,512]{1,0:T(8,128)(2,1)}, u32[]{:S(2)}) %copy-start.2) | copy-done | bytes 524312
  3.7 0.0 copy-start.3
  3.7 1.0 %copy-done.3 = bf16[3,256,256]{2,1,0:T(8,128)(2,1)S(1)} copy-done((bf16[3,256,256]{2,1,0:T(8,128)(2,1)S(1)}, bf16[3,256,256]{2,1,0:T(8,128)(2,1)}, u32[]{:S(2)}) %copy-start.3) | copy-done | bytes 393240
  4.7 0.0 copy-start.4
  4.7 1.0 %copy-done.4 = bf16[3,3,64,256]{3,2,1,0:T(8,128)(2,1)S(1)} copy-done((bf16[3,3,64,256]{3,2,1,0:T(8,128)(2,1)S(1)}, bf16[3,3,64,256]{3,2,1,0:T(8,128)(2,1)}, u32[]{:S(2)}) %copy-start.4) | copy-done | bytes 294936
  5.6 0.0 copy-start.5
  5.6 0.9 %copy-done.5 = bf16[2,4,64,256]{3,2,1,0:T(8,128)(2,1)S(1)} copy-done((bf16[2,4,64,256]{3,2,1,0:T(8,128)(2,1)S(1)}, bf16[2,4,64,256]{3,2,1,0:T(8,128)(2,1)}, u32[]{:S(2)}) %copy-start.5) | copy-done | bytes 262168
  6.6 0.0 copy-start.6
  6.6 0.7 %copy-done.6 = f32[256]{0:T(256)S(1)} copy-done((f32[256]{0:T(256)S(1)}, f32[256]{0:T(256)}, u32[]{:S(2)}) %copy-start.6) | copy-done | bytes 1048
  7.3 0.0 copy-start.7
  7.3 0.9 %copy-done.7 = bf16[256,256]{1,0:T(8,128)(2,1)S(1)} copy-done((bf16[256,256]{1,0:T(8,128)(2,1)S(1)}, bf16[256,256]{1,0:T(8,128)(2,1)}, u32[]{:S(2)}) %copy-start.7) | copy-done | bytes 131096
  8.2 0.0 copy-start.8
  8.2 0.9 %copy-done.8 = bf16[256,256]{1,0:T(8,128)(2,1)S(1)} copy-done((bf16[256,256]{1,0:T(8,128)(2,1)S(1)}, bf16[256,256]{1,0:T(8,128)(2,1)}, u32[]{:S(2)}) %copy-start.8) | copy-done | bytes 131096
  9.1 24.1 %shard_map.91 = bf16[1,2,32,512]{3,2,1,0:T(8,128)(2,1)S(1)} custom-call(bf16[2,4,64,256]{3,2,1,0:T(8,128)(2,1)S(1)} %copy-done.5, f32[1,256]{1,0:T(1,128)S(1)} %bitcast.1, bf16[3,3,64,256]{3,2,1,0:T(8,128)(2,1)S(1)} %copy-done.4, bf16[3,256,256]{2,1,0:T(8,128)(2,1)S(1)} %copy-done.3, bf16[2048,512]{1,0:T(8,128)(2,1)S(1)} %copy-done, ...), custom_call_target="tpu_custom_call" | custom-call | flops 2000000000 | bytes 5000000 | tf_op jit(solution)/shard_map/pallas_call | solution.py:280
  33.2 0.6 %copy.11 = bf16[1,2,32,512]{3,2,1,0:T(8,128)(2,1)} copy(bf16[1,2,32,512]{3,2,1,0:T(8,128)(2,1)S(1)} %shard_map.91) | data formatting | bytes 131072
Async XLA Ops:
  0.0 1.6 %copy-start = (bf16[2048,512]{1,0:T(8,128)(2,1)S(1)}, bf16[2048,512]{1,0:T(8,128)(2,1)}, u32[]{:S(2)}) copy-start(bf16[2048,512]{1,0:T(8,128)(2,1)} %hw.1) | copy-start | bytes 6291460
  1.6 1.0 %copy-start.1 = (bf16[512,512]{1,0:T(8,128)(2,1)S(1)}, bf16[512,512]{1,0:T(8,128)(2,1)}, u32[]{:S(2)}) copy-start(bf16[512,512]{1,0:T(8,128)(2,1)} %qw.1) | copy-start | bytes 1572868
  2.6 1.0 %copy-start.2 = (bf16[512,512]{1,0:T(8,128)(2,1)S(1)}, bf16[512,512]{1,0:T(8,128)(2,1)}, u32[]{:S(2)}) copy-start(bf16[512,512]{1,0:T(8,128)(2,1)} %kw.1) | copy-start | bytes 1572868
  3.7 1.0 %copy-start.3 = (bf16[3,256,256]{2,1,0:T(8,128)(2,1)S(1)}, bf16[3,256,256]{2,1,0:T(8,128)(2,1)}, u32[]{:S(2)}) copy-start(bf16[3,256,256]{2,1,0:T(8,128)(2,1)} %tw.1) | copy-start | bytes 1179652
  4.7 1.0 %copy-start.4 = (bf16[3,3,64,256]{3,2,1,0:T(8,128)(2,1)S(1)}, bf16[3,3,64,256]{3,2,1,0:T(8,128)(2,1)}, u32[]{:S(2)}) copy-start(bf16[3,3,64,256]{3,2,1,0:T(8,128)(2,1)} %sw.1) | copy-start | bytes 884740
  5.6 0.9 %copy-start.5 = (bf16[2,4,64,256]{3,2,1,0:T(8,128)(2,1)S(1)}, bf16[2,4,64,256]{3,2,1,0:T(8,128)(2,1)}, u32[]{:S(2)}) copy-start(bf16[2,4,64,256]{3,2,1,0:T(8,128)(2,1)} %video.1) | copy-start | bytes 786436
  6.6 0.7 %copy-start.6 = (f32[256]{0:T(256)S(1)}, f32[256]{0:T(256)}, u32[]{:S(2)}) copy-start(f32[256]{0:T(256)} %param.10) | copy-start | bytes 3076
  7.3 0.9 %copy-start.7 = (bf16[256,256]{1,0:T(8,128)(2,1)S(1)}, bf16[256,256]{1,0:T(8,128)(2,1)}, u32[]{:S(2)}) copy-start(bf16[256,256]{1,0:T(8,128)(2,1)} %constant.5.clone.haar) | copy-start | bytes 393220
  8.2 0.9 %copy-start.8 = (bf16[256,256]{1,0:T(8,128)(2,1)S(1)}, bf16[256,256]{1,0:T(8,128)(2,1)}, u32[]{:S(2)}) copy-start(bf16[256,256]{1,0:T(8,128)(2,1)} %constant.4.clone.heads) | copy-start | bytes 393220

commit v2 on v1

--- a/solution.py
+++ b/solution.py
@@ -276,7 +276,7 @@
     haar = jnp.asarray(haar_matrix(cols), bf16)
     total, places = frames + 2, rows // 2 * (cols // 2)
     dma = pltpu.SemaphoreType.DMA
-    anywhere, vmem = pl.BlockSpec(memory_space=pl.ANY), pl.BlockSpec(memory_space=pltpu.VMEM)
+    anywhere, vmem = pl.BlockSpec(memory_space=pltpu.HBM), pl.BlockSpec(memory_space=pltpu.VMEM)
     return pl.pallas_call(
         functools.partial(kernel, nh, nt),
         out_shape=jax.ShapeDtypeStruct((frames // 2, rows // 2, cols // 2, width), bf16),
@@ -304,7 +304,7 @@
             dma((nt,)), dma((nt,)),
         ],
         compiler_params=pltpu.CompilerParams(
-            collective_id=0, has_side_effects=True, vmem_limit_bytes=40 * 1024 * 1024
+            collective_id=0, has_side_effects=True, vmem_limit_bytes=60 * 1024 * 1024
         ),
         cost_estimate=pl.CostEstimate(
             flops=2 * 10**9, bytes_accessed=5 * 10**6, transcendentals=10**6

time: 34.3 us -> 26.5 us (0.77)
  local copies, waits for them, and re-layouts: 9.7 us -> 1.47 us
  Pallas kernels: 24.1 us -> 24.8 us
    unnamed x19 -> x1, local copies, waits for them, and re-layouts: 9.7 us -> 1.47 us
    pallas_call x1, Pallas kernels: 24.1 us -> 24.8 us  [body(): pl.pallas_call(functools.partial(kernel, nh, nt), out_shape=jax.ShapeDtyp...]
where the time goes in v2:
time: 26.5 us; the launch traced here: 26.3 us
  Pallas kernels  24.8 us (94%)
  local copies, waits for them, and re-layouts  1.47 us (6%)
    pallas_call x1, Pallas kernels, body(): pl.pallas_call(functools.partial(kernel, nh, nt), out_shape=jax.ShapeDtyp...  24.8 us
    unnamed x1, local copies, waits for them, and re-layouts  1.47 us

profile of v2, /device:TPU:28, one launch (start us, length us, event | category | flops | bytes accessed | tf_op | source)
XLA Modules:
  0.0 26.3 jit_solution(7735377919662395125)
XLA Ops:
  0.0 24.8 %shard_map.91 = bf16[1,2,32,512]{3,2,1,0:T(8,128)(2,1)} custom-call(bf16[2,4,64,256]{3,2,1,0:T(8,128)(2,1)} %video.1, f32[1,256]{1,0:T(1,128)} %bitcast.1, bf16[3,3,64,256]{3,2,1,0:T(8,128)(2,1)} %sw.1, bf16[3,256,256]{2,1,0:T(8,128)(2,1)} %tw.1, bf16[2048,512]{1,0:T(8,128)(2,1)} %hw.1, bf16[512,512]{1,0:T(8,128)(2,1)} %qw.1, bf16[512,512]{1,0:T(8,128)(2,1)} %kw.1, ...), custom_call_target="tpu_custom_call" | custom-call | flops 2000000000 | bytes 5000000 | tf_op jit(solution)/shard_map/pallas_call | solution.py:280
  24.8 1.5 %copy.11 = bf16[1,2,32,512]{3,2,1,0:T(8,128)(2,1)} copy(bf16[1,2,32,512]{3,2,1,0:T(8,128)(2,1)} %shard_map.91) | data formatting | bytes 131072

commit v3 on v2

--- a/solution.py
+++ b/solution.py
@@ -219,7 +219,7 @@
         shares.append(
             remote(gl.at[0], gl.at[d], lsend.at[d], lrecv.at[d], tm=lax.rem(t + d, nt))
         )
-    for d in range(1, nt):
+    for d in range(nt - 1, 0, -1):
         pl.when(t + d < nt)(shares[d].start)
 
     local[5].wait()
@@ -304,7 +304,7 @@
             dma((nt,)), dma((nt,)),
         ],
         compiler_params=pltpu.CompilerParams(
-            collective_id=0, has_side_effects=True, vmem_limit_bytes=60 * 1024 * 1024
+            collective_id=0, has_side_effects=True, vmem_limit_bytes=40 * 1024 * 1024
         ),
         cost_estimate=pl.CostEstimate(
             flops=2 * 10**9, bytes_accessed=5 * 10**6, transcendentals=10**6

time: 26.5 us -> 34.8 us (1.31)
  the two profiles are of different devices: /device:TPU:28 before, /device:TPU:21 now
where the time goes in v3:
time: 34.8 us; the launch traced here: 34.4 us
  Pallas kernels  24.7 us (71%)
  local copies, waits for them, and re-layouts  9.7 us (28%)
    pallas_call x1, Pallas kernels, body(): pl.pallas_call(functools.partial(kernel, nh, nt), out_shape=jax.ShapeDtyp...  24.7 us
    unnamed x19, local copies, waits for them, and re-layouts  9.7 us

profile of v3, /device:TPU:21, one launch (start us, length us, event | category | flops | bytes accessed | tf_op | source)
XLA Modules:
  0.0 34.4 jit_solution(589263803445685703)
XLA Ops:
  0.0 0.0 copy-start
  0.0 1.6 %copy-done = bf16[2048,512]{1,0:T(8,128)(2,1)S(1)} copy-done((bf16[2048,512]{1,0:T(8,128)(2,1)S(1)}, bf16[2048,512]{1,0:T(8,128)(2,1)}, u32[]{:S(2)}) %copy-start) | copy-done | bytes 2097176
  1.6 0.0 copy-start.1
  1.6 1.0 %copy-done.1 = bf16[512,512]{1,0:T(8,128)(2,1)S(1)} copy-done((bf16[512,512]{1,0:T(8,128)(2,1)S(1)}, bf16[512,512]{1,0:T(8,128)(2,1)}, u32[]{:S(2)}) %copy-start.1) | copy-done | bytes 524312
  2.6 0.0 copy-start.2
  2.6 1.0 %copy-done.2 = bf16[512,512]{1,0:T(8,128)(2,1)S(1)} copy-done((bf16[512,512]{1,0:T(8,128)(2,1)S(1)}, bf16[512,512]{1,0:T(8,128)(2,1)}, u32[]{:S(2)}) %copy-start.2) | copy-done | bytes 524312
  3.7 0.0 copy-start.3
  3.7 1.0 %copy-done.3 = bf16[3,256,256]{2,1,0:T(8,128)(2,1)S(1)} copy-done((bf16[3,256,256]{2,1,0:T(8,128)(2,1)S(1)}, bf16[3,256,256]{2,1,0:T(8,128)(2,1)}, u32[]{:S(2)}) %copy-start.3) | copy-done | bytes 393240
  4.7 0.0 copy-start.4
  4.7 1.0 %copy-done.4 = bf16[3,3,64,256]{3,2,1,0:T(8,128)(2,1)S(1)} copy-done((bf16[3,3,64,256]{3,2,1,0:T(8,128)(2,1)S(1)}, bf16[3,3,64,256]{3,2,1,0:T(8,128)(2,1)}, u32[]{:S(2)}) %copy-start.4) | copy-done | bytes 294936
  5.6 0.0 copy-start.5
  5.6 0.9 %copy-done.5 = bf16[2,4,64,256]{3,2,1,0:T(8,128)(2,1)S(1)} copy-done((bf16[2,4,64,256]{3,2,1,0:T(8,128)(2,1)S(1)}, bf16[2,4,64,256]{3,2,1,0:T(8,128)(2,1)}, u32[]{:S(2)}) %copy-start.5) | copy-done | bytes 262168
  6.6 0.0 copy-start.6
  6.6 0.7 %copy-done.6 = f32[256]{0:T(256)S(1)} copy-done((f32[256]{0:T(256)S(1)}, f32[256]{0:T(256)}, u32[]{:S(2)}) %copy-start.6) | copy-done | bytes 1048
  7.3 0.0 copy-start.7
  7.3 0.9 %copy-done.7 = bf16[256,256]{1,0:T(8,128)(2,1)S(1)} copy-done((bf16[256,256]{1,0:T(8,128)(2,1)S(1)}, bf16[256,256]{1,0:T(8,128)(2,1)}, u32[]{:S(2)}) %copy-start.7) | copy-done | bytes 131096
  8.2 0.0 copy-start.8
  8.2 0.9 %copy-done.8 = bf16[256,256]{1,0:T(8,128)(2,1)S(1)} copy-done((bf16[256,256]{1,0:T(8,128)(2,1)S(1)}, bf16[256,256]{1,0:T(8,128)(2,1)}, u32[]{:S(2)}) %copy-start.8) | copy-done | bytes 131096
  9.1 24.7 %shard_map.91 = bf16[1,2,32,512]{3,2,1,0:T(8,128)(2,1)S(1)} custom-call(bf16[2,4,64,256]{3,2,1,0:T(8,128)(2,1)S(1)} %copy-done.5, f32[1,256]{1,0:T(1,128)S(1)} %bitcast.1, bf16[3,3,64,256]{3,2,1,0:T(8,128)(2,1)S(1)} %copy-done.4, bf16[3,256,256]{2,1,0:T(8,128)(2,1)S(1)} %copy-done.3, bf16[2048,512]{1,0:T(8,128)(2,1)S(1)} %copy-done, ...), custom_call_target="tpu_custom_call" | custom-call | flops 2000000000 | bytes 5000000 | tf_op jit(solution)/shard_map/pallas_call | solution.py:280
  33.8 0.6 %copy.11 = bf16[1,2,32,512]{3,2,1,0:T(8,128)(2,1)} copy(bf16[1,2,32,512]{3,2,1,0:T(8,128)(2,1)S(1)} %shard_map.91) | data formatting | bytes 131072
Async XLA Ops:
  0.0 1.6 %copy-start = (bf16[2048,512]{1,0:T(8,128)(2,1)S(1)}, bf16[2048,512]{1,0:T(8,128)(2,1)}, u32[]{:S(2)}) copy-start(bf16[2048,512]{1,0:T(8,128)(2,1)} %hw.1) | copy-start | bytes 6291460
  1.6 1.0 %copy-start.1 = (bf16[512,512]{1,0:T(8,128)(2,1)S(1)}, bf16[512,512]{1,0:T(8,128)(2,1)}, u32[]{:S(2)}) copy-start(bf16[512,512]{1,0:T(8,128)(2,1)} %qw.1) | copy-start | bytes 1572868
  2.6 1.0 %copy-start.2 = (bf16[512,512]{1,0:T(8,128)(2,1)S(1)}, bf16[512,512]{1,0:T(8,128)(2,1)}, u32[]{:S(2)}) copy-start(bf16[512,512]{1,0:T(8,128)(2,1)} %kw.1) | copy-start | bytes 1572868
  3.7 1.0 %copy-start.3 = (bf16[3,256,256]{2,1,0:T(8,128)(2,1)S(1)}, bf16[3,256,256]{2,1,0:T(8,128)(2,1)}, u32[]{:S(2)}) copy-start(bf16[3,256,256]{2,1,0:T(8,128)(2,1)} %tw.1) | copy-start | bytes 1179652
  4.7 1.0 %copy-start.4 = (bf16[3,3,64,256]{3,2,1,0:T(8,128)(2,1)S(1)}, bf16[3,3,64,256]{3,2,1,0:T(8,128)(2,1)}, u32[]{:S(2)}) copy-start(bf16[3,3,64,256]{3,2,1,0:T(8,128)(2,1)} %sw.1) | copy-start | bytes 884740
  5.6 0.9 %copy-start.5 = (bf16[2,4,64,256]{3,2,1,0:T(8,128)(2,1)S(1)}, bf16[2,4,64,256]{3,2,1,0:T(8,128)(2,1)}, u32[]{:S(2)}) copy-start(bf16[2,4,64,256]{3,2,1,0:T(8,128)(2,1)} %video.1) | copy-start | bytes 786436
  6.6 0.7 %copy-start.6 = (f32[256]{0:T(256)S(1)}, f32[256]{0:T(256)}, u32[]{:S(2)}) copy-start(f32[256]{0:T(256)} %param.10) | copy-start | bytes 3076
  7.3 0.9 %copy-start.7 = (bf16[256,256]{1,0:T(8,128)(2,1)S(1)}, bf16[256,256]{1,0:T(8,128)(2,1)}, u32[]{:S(2)}) copy-start(bf16[256,256]{1,0:T(8,128)(2,1)} %constant.5.clone.haar) | copy-start | bytes 393220
  8.2 0.9 %copy-start.8 = (bf16[256,256]{1,0:T(8,128)(2,1)S(1)}, bf16[256,256]{1,0:T(8,128)(2,1)}, u32[]{:S(2)}) copy-start(bf16[256,256]{1,0:T(8,128)(2,1)} %constant.4.clone.heads) | copy-start | bytes 393220

commit v4 on v2

--- a/solution.py
+++ b/solution.py
@@ -25,11 +25,12 @@
 
 
 def kernel(
-    nh, nt, video, gain, sw, tw, hw, qw, kw, haar, heads, out,
+    nh, nt, ng, video, gain, sw, tw, hw, qw, kw, haar, heads, out,
     vid, wfull, twv, hwv, qwv, kwv, haarv, headsv, patches, acc, sp, mg, bands, gl, sc,
     local_sem, wsend, wrecv, fsend, frecv, hsend, hrecv, gsend, grecv, vsend, vrecv, lsend, lrecv,
+    asend, arecv, ssend, srecv,
 ):
-    h, t = lax.axis_index("height"), lax.axis_index("tm")
+    h, t, g = lax.axis_index("height"), lax.axis_index("tm"), lax.axis_index("groups")
     frames, rows, cols, chan = video.shape
     cin = sw.shape[2]
     chips = nh // 2
@@ -62,6 +63,9 @@
     for d in range(1, nt):
         pl.semaphore_signal(barrier, inc=1, device_id={"tm": lax.rem(t + d, nt)}, device_id_type=MESH)
 
+    for d in range(1, ng):
+        pl.semaphore_signal(barrier, inc=1, device_id={"groups": lax.rem(g + d, ng)}, device_id_type=MESH)
+
     total = frames + 2
     for edge, slot in ((0, 0), (nh - 1, rows + 1)):
         @pl.when(h == edge)
@@ -78,7 +82,7 @@
         def _():
             gl[d] = jnp.zeros(gl.shape[1:], bf16)
 
-    pl.semaphore_wait(barrier, nh - 1 + nt - 1)
+    pl.semaphore_wait(barrier, nh - 1 + nt - 1 + ng - 1)
 
     later = {"tm": lax.rem(t + 1, nt)}
     above, below = {"height": lax.rem(h + nh - 1, nh)}, {"height": lax.rem(h + 1, nh)}
@@ -104,20 +108,46 @@
     sends = (up, down)
     receives = (down, up)
 
-    weights, onward = {}, {}
+    part = cin // ng
+    weights, onward, across, second = {}, {}, {}, {}
     for a in range(3):
-        piece = wfull.at[a, :, own_in, :]
         weights[0, a] = remote(
-            sw.at[a], piece, wsend.at[0, a], wrecv.at[0, a], height=sibling
+            sw.at[a], wfull.at[a, :, own_in, :], wsend.at[0, a], wrecv.at[0, a], height=sibling
         )
         for d in range(1, chips):
+            mine_in = pl.ds(pl.multiple_of(h * cin + g * part, part), part)
             weights[d, a] = remote(
-                sw.at[a], piece, wsend.at[d, a], wrecv.at[d, a],
-                height=lax.rem(chip + d, chips) * 2 + core,
+                sw.at[a, :, pl.ds(pl.multiple_of(g * part, part), part), :], wfull.at[a, :, mine_in, :],
+                wsend.at[d, a], wrecv.at[d, a], height=lax.rem(chip + d, chips) * 2 + core,
             )
             origin = lax.rem(chip + chips - d, chips) * 2 + core
-            held = wfull.at[a, :, pl.ds(pl.multiple_of(origin * cin, cin), cin), :]
-            onward[d, a] = remote(held, held, fsend.at[d, a], frecv.at[d, a], height=sibling)
+            for e in range(ng):
+                source = lax.rem(g + ng - e, ng)
+                start = pl.multiple_of(origin * cin + source * part, part)
+                held = wfull.at[a, :, pl.ds(start, part), :]
+                if e == 0:
+                    first = held
+                    onward[d, a] = remote(held, held, fsend.at[d, a], frecv.at[d, a], height=sibling)
+                else:
+                    across[d, a, e] = remote(
+                        first, first, asend.at[d, a, e], arecv.at[d, a, e], groups=lax.rem(g + e, ng)
+                    )
+                    second[d, a, e] = remote(
+                        held, held, ssend.at[d, a, e], srecv.at[d, a, e], height=sibling
+                    )
+
+    def relay_first(a):
+        for d in range(1, chips):
+            weights[d, a].wait_recv()
+            for e in range(1, ng):
+                across[d, a, e].start()
+            onward[d, a].start()
+
+    def relay_second(a):
+        for d in range(1, chips):
+            for e in range(1, ng):
+                across[d, a, e].wait_recv()
+                second[d, a, e].start()
 
     for cond, copy in zip(sends, halo):
         pl.when(cond)(copy.start)
@@ -160,25 +190,22 @@
     for i, row in ((0, rows + 1), (1, 0)):
         pl.when(receives[i])(halo[i].wait_recv)
         activate_rows(2, frames, row, 1)
-    for d in range(1, chips):
-        weights[d, 0].wait_recv()
-        onward[d, 0].start()
+    relay_first(0)
+    relay_first(1)
+    relay_second(0)
+    relay_first(2)
+    relay_second(1)
     pl.when(has_past)(past[2].wait_recv)
     activate_rows(0, 2, 1, rows)
-    for d in range(1, chips):
-        weights[d, 1].wait_recv()
-        onward[d, 1].start()
+    relay_second(2)
     for i, row in ((0, rows + 1), (1, 0)):
         pl.when(has_past & receives[i])(relay[i].wait_recv)
         activate_rows(0, 2, row, 1)
     local[1].wait()
     for a in range(3):
-        if a == 1:
-            for d in range(1, chips):
-                weights[d, 2].wait_recv()
-                onward[d, 2].start()
         weights[0, a].wait_recv()
         receive([onward[d, a] for d in range(1, chips)])
+        receive([second[d, a, e] for d in range(1, chips) for e in range(1, ng)])
         taps = wfull[a].reshape(3 * chan, wfull.shape[3])
         for f in range(total):
             part = jnp.dot(
@@ -260,13 +287,13 @@
         pl.when(has_past & sends[i])(relay[i].wait_send)
     for copy in past:
         pl.when(has_next)(copy.wait_send)
-    for copy in list(weights.values()) + list(onward.values()):
+    for copy in [c for group in (weights, onward, across, second) for c in group.values()]:
         copy.wait_send()
     for d in range(1, nt):
         pl.when(t + d < nt)(shares[d].wait_send)
 
 
-def body(nh, nt, video, norm_gain, sw, tw, hw, qw, kw):
+def body(nh, nt, ng, video, norm_gain, sw, tw, hw, qw, kw):
     frames, rows, cols, chan = video.shape
     outward, width = sw.shape[3], hw.shape[1]
     bf16, f32 = jnp.bfloat16, jnp.float32
@@ -278,7 +305,7 @@
     dma = pltpu.SemaphoreType.DMA
     anywhere, vmem = pl.BlockSpec(memory_space=pltpu.HBM), pl.BlockSpec(memory_space=pltpu.VMEM)
     return pl.pallas_call(
-        functools.partial(kernel, nh, nt),
+        functools.partial(kernel, nh, nt, ng),
         out_shape=jax.ShapeDtypeStruct((frames // 2, rows // 2, cols // 2, width), bf16),
         in_specs=[anywhere, vmem] + [anywhere] * 7,
         out_specs=vmem,
@@ -302,6 +329,7 @@
             dma((nh // 2, 3)), dma((nh // 2, 3)), dma((nh // 2, 3)), dma((nh // 2, 3)),
             dma((2,)), dma((2,)), dma((2,)), dma((2,)), dma((3,)), dma((3,)),
             dma((nt,)), dma((nt,)),
+            dma((nh // 2, 3, ng)), dma((nh // 2, 3, ng)), dma((nh // 2, 3, ng)), dma((nh // 2, 3, ng)),
         ],
         compiler_params=pltpu.CompilerParams(
             collective_id=0, has_side_effects=True, vmem_limit_bytes=60 * 1024 * 1024
@@ -323,5 +351,5 @@
         P(),
     )
     out_specs = P(("groups", "tm"), "height", None, None)
-    run = functools.partial(body, mesh.shape["height"], mesh.shape["tm"])
+    run = functools.partial(body, mesh.shape["height"], mesh.shape["tm"], mesh.shape["groups"])
     return jax.shard_map(run, mesh=mesh, in_specs=in_specs, out_specs=out_specs, check_vma=False)

time: 26.5 us -> 29.9 us (1.13)
  Pallas kernels: 24.8 us -> 28.3 us
    pallas_call x1, Pallas kernels: 24.8 us -> 28.3 us  [body(): pl.pallas_call(functools.partial(kernel, nh, nt, ng), out_shape=jax.Shape...]
where the time goes in v4:
time: 29.9 us; the launch traced here: 29.8 us
  Pallas kernels  28.3 us (95%)
  local copies, waits for them, and re-layouts  1.47 us (5%)
    pallas_call x1, Pallas kernels, body(): pl.pallas_call(functools.partial(kernel, nh, nt, ng), out_shape=jax.Shape...  28.3 us
    unnamed x1, local copies, waits for them, and re-layouts  1.47 us

profile of v4, /device:TPU:28, one launch (start us, length us, event | category | flops | bytes accessed | tf_op | source)
XLA Modules:
  0.0 29.8 jit_solution(1244510704449257245)
XLA Ops:
  0.0 28.3 %shard_map.91 = bf16[1,2,32,512]{3,2,1,0:T(8,128)(2,1)} custom-call(bf16[2,4,64,256]{3,2,1,0:T(8,128)(2,1)} %video.1, f32[1,256]{1,0:T(1,128)} %bitcast.1, bf16[3,3,64,256]{3,2,1,0:T(8,128)(2,1)} %sw.1, bf16[3,256,256]{2,1,0:T(8,128)(2,1)} %tw.1, bf16[2048,512]{1,0:T(8,128)(2,1)} %hw.1, bf16[512,512]{1,0:T(8,128)(2,1)} %qw.1, bf16[512,512]{1,0:T(8,128)(2,1)} %kw.1, ...), custom_call_target="tpu_custom_call" | custom-call | flops 2000000000 | bytes 5000000 | tf_op jit(solution)/shard_map/pallas_call | solution.py:307
  28.3 1.5 %copy.11 = bf16[1,2,32,512]{3,2,1,0:T(8,128)(2,1)} copy(bf16[1,2,32,512]{3,2,1,0:T(8,128)(2,1)} %shard_map.91) | data formatting | bytes 131072

commit v5 on v2

--- a/solution.py
+++ b/solution.py
@@ -119,14 +119,14 @@
             held = wfull.at[a, :, pl.ds(pl.multiple_of(origin * cin, cin), cin), :]
             onward[d, a] = remote(held, held, fsend.at[d, a], frecv.at[d, a], height=sibling)
 
+    for a in range(3):
+        for d in range(1, chips):
+            weights[d, a].start()
+        weights[0, a].start()
     for cond, copy in zip(sends, halo):
         pl.when(cond)(copy.start)
     for copy in past:
         pl.when(has_next)(copy.start)
-    for a in range(3):
-        for d in range(1, chips):
-            weights[d, a].start()
-        weights[0, a].start()
 
     column = lax.broadcasted_iota(jnp.int32, (cols, chan), 0)
     scale = gain[...]
@@ -163,11 +163,11 @@
     for d in range(1, chips):
         weights[d, 0].wait_recv()
         onward[d, 0].start()
-    pl.when(has_past)(past[2].wait_recv)
-    activate_rows(0, 2, 1, rows)
     for d in range(1, chips):
         weights[d, 1].wait_recv()
         onward[d, 1].start()
+    pl.when(has_past)(past[2].wait_recv)
+    activate_rows(0, 2, 1, rows)
     for i, row in ((0, rows + 1), (1, 0)):
         pl.when(has_past & receives[i])(relay[i].wait_recv)
         activate_rows(0, 2, row, 1)

time: 26.5 us -> 27.4 us (1.034)
  Pallas kernels: 24.8 us -> 25.8 us
    pallas_call x1, Pallas kernels: 24.8 us -> 25.8 us  [body(): pl.pallas_call(functools.partial(kernel, nh, nt), out_shape=jax.ShapeDtyp...]
where the time goes in v5:
time: 27.4 us; the launch traced here: 27.2 us
  Pallas kernels  25.8 us (94%)
  local copies, waits for them, and re-layouts  1.47 us (5%)
    pallas_call x1, Pallas kernels, body(): pl.pallas_call(functools.partial(kernel, nh, nt), out_shape=jax.ShapeDtyp...  25.8 us
    unnamed x1, local copies, waits for them, and re-layouts  1.47 us

profile of v5, /device:TPU:28, one launch (start us, length us, event | category | flops | bytes accessed | tf_op | source)
XLA Modules:
  0.0 27.2 jit_solution(7365697654633758743)
XLA Ops:
  0.0 25.8 %shard_map.91 = bf16[1,2,32,512]{3,2,1,0:T(8,128)(2,1)} custom-call(bf16[2,4,64,256]{3,2,1,0:T(8,128)(2,1)} %video.1, f32[1,256]{1,0:T(1,128)} %bitcast.1, bf16[3,3,64,256]{3,2,1,0:T(8,128)(2,1)} %sw.1, bf16[3,256,256]{2,1,0:T(8,128)(2,1)} %tw.1, bf16[2048,512]{1,0:T(8,128)(2,1)} %hw.1, bf16[512,512]{1,0:T(8,128)(2,1)} %qw.1, bf16[512,512]{1,0:T(8,128)(2,1)} %kw.1, ...), custom_call_target="tpu_custom_call" | custom-call | flops 2000000000 | bytes 5000000 | tf_op jit(solution)/shard_map/pallas_call | solution.py:280
  25.8 1.5 %copy.11 = bf16[1,2,32,512]{3,2,1,0:T(8,128)(2,1)} copy(bf16[1,2,32,512]{3,2,1,0:T(8,128)(2,1)} %shard_map.91) | data formatting | bytes 131072
